TPU v7x, 128 devices: a whole 4x4x4 slice. The times are simulated.
128 devices in a mesh: mem: 8 (over y, x_lo), grid: 16 (over z, x_hi, core).
Axes of the slice: x: 4 (x_hi: 2, x_lo: 2; x = x_hi * 2 + x_lo), y: 4, z: 4, core: 2. Of those that a mesh axis runs over, the one named last changes fastest.
Arguments:
- gradient: float32 [16, 256, 512], P('mem', 'grid'), may hold values from -6 to 6
- members: bfloat16 [128, 16, 256, 512], P('mem', None, 'grid'), may hold values from -6 to 6
- eof_basis: float32 [16, 16], replicated, may hold values from -1.5 to 1.5
- spectral_weight: float32 [16, 128, 256], P(None, None, 'grid'), may hold values from 0.5 to 4
- retained: int32 [16], replicated, may hold values from 32 to 255
- mode_count: int32 [1], replicated, may hold values from 8 to 16
Outputs:
- increment: float32 [16, 256, 512], P('mem', 'grid')
- control: float32 [128, 16, 128, 256], P('mem', None, None, 'grid')
All inputs are finite; a program needn't handle non-finite values.
Results may differ from a plain program's by a relative error of at most 0.0003.
Values may be sent and summed in bfloat16 or wider, within the bound.
No kernel may reach another device: no remote copies, remote signals or barrier semaphores. Data moves between devices by JAX's collectives and lax.ppermute only.
A program may use at most 192 MiB of HBM per device.

v0:
```python
import math

import jax
import jax.numpy as jnp
from jax import lax
from jax.sharding import PartitionSpec as P


def cosine_table(length, retain_count):
    cells = jnp.arange(length, dtype=jnp.float32)
    waves = jnp.arange(retain_count, dtype=jnp.float32)
    factor = jnp.where(waves == 0.0, math.sqrt(1.0 / length), math.sqrt(2.0 / length))
    return jnp.cos(math.pi * (cells[:, None] + 0.5) * waves[None, :] / length) * factor[None, :]


def band_filter(weight, retained):
    y_wave = jnp.arange(weight.shape[1], dtype=jnp.int32)[:, None]
    x_wave = jnp.arange(weight.shape[2], dtype=jnp.int32)[None, :]
    inside = (y_wave + x_wave)[None, :, :] < retained[:, None, None]
    return weight * inside.astype(jnp.float32)


def local(gradient, members, eof_basis, spectral_weight, retained, mode_count):
    high = lax.Precision.HIGHEST
    grid_count = lax.axis_size("grid")
    group_count = lax.axis_size("mem")
    member_total = members.shape[0] * group_count
    member_scale = 1.0 / math.sqrt(member_total - 1)
    levels = lax.all_gather(gradient, "mem", axis=0, tiled=True)
    level_count, row_count, columns = levels.shape
    mode_total = eof_basis.shape[1]
    y_kept = spectral_weight.shape[1]
    kx_local = spectral_weight.shape[2]
    x_table = cosine_table(columns, kx_local * grid_count)
    y_table = cosine_table(row_count * grid_count, y_kept)
    basis = eof_basis * (jnp.arange(mode_total) < mode_count[0]).astype(jnp.float32)[None, :]
    whole_grad = lax.all_gather(levels, "grid", axis=1, tiled=True)
    weight_whole = lax.all_gather(spectral_weight, "grid", axis=2, tiled=True)
    spectral_filter = band_filter(weight_whole, retained)
    owned = lax.all_to_all(members, "grid", split_axis=0, concat_axis=2, tiled=True)
    values = owned.astype(jnp.float32)
    product = values * whole_grad[None]
    projected = jnp.einsum("zk,mzyx->mkyx", basis, product, precision=high)
    x_spectrum = jnp.einsum("mkyx,xp->mkyp", projected, x_table, precision=high)
    local_control = (
        jnp.einsum("yq,mkyp->mkqp", y_table, x_spectrum, precision=high)
        * spectral_filter[None]
        * member_scale
    )
    y_back = jnp.einsum(
        "yq,mkqp->mkyp", y_table, local_control * spectral_filter[None], precision=high
    )
    x_back = jnp.einsum("mkyp,xp->mkyx", y_back, x_table, precision=high)
    vertical = jnp.einsum("zk,mkyx->mzyx", basis, x_back, precision=high)
    partial_value = jnp.sum(values * vertical * member_scale, axis=0)
    control = lax.all_to_all(local_control, "grid", split_axis=3, concat_axis=0, tiled=True)
    level_share = level_count // group_count
    blocks = partial_value.reshape(group_count, level_share, grid_count, row_count, columns)
    blocks = blocks.transpose(0, 2, 1, 3, 4).reshape(
        group_count * grid_count, level_share, row_count, columns
    )
    increment = lax.psum_scatter(blocks, ("mem", "grid"), scatter_dimension=0, tiled=True)[0]
    return (increment, control)


def solution(mesh):
    return jax.shard_map(
        local,
        mesh=mesh,
        in_specs=(
            P("mem", "grid", None),
            P("mem", None, "grid", None),
            P(),
            P(None, None, "grid"),
            P(),
            P(),
        ),
        out_specs=(P("mem", "grid", None), P("mem", None, None, "grid")),
        check_vma=False,
    )
```

profile of v0, /device:TPU:0, one launch (start us, length us, event | category | flops | bytes accessed | tf_op | source)
XLA Modules:
  0.0 939.2 jit_solution(17248173704263066993)
XLA Ops:
  7.2 32.5 %all_gather.9 = f32[16,16,512]{2,1,0:T(8,128)} all-gather(f32[2,16,512]{2,1,0:T(8,128)} %param.6), channel_id=1, replica_groups=mesh['mem'=8,'grid'=16] {'mem'}, dimensions={0}, use_global_device_ids=true | all-gather | bytes 589824 | tf_op jit(solution)/shard_map/all_gather | solution.py:29
  39.7 8.0 all-to-all-start
  47.8 0.0 all-gather.5.cloned.1.call-start
  47.8 0.7 all-gather.5.cloned.1.call-update
  48.6 0.0 reduce-scatter.2.cloned.1.call-start
  49.3 56.5 %all-to-all-done = bf16[16,16,16,512]{3,2,1,0:T(8,128)(2,1)} async-done(((bf16[16,16,16,512]{3,2,1,0:T(8,128)(2,1)}), bf16[16,16,16,512]{3,2,1,0:T(8,128)(2,1)}, u32[]{:S(2)}, u32[]{:S(2)}) %all-to-all-start) | async-done | bytes 4194336 | tf_op jit(solution)/shard_map/all_to_all | solution.py:40
  105.9 7.7 bitcast_convert_fusion
  113.5 10.0 %copy.20 = f32[1,16,16,16,512]{4,1,3,2,0:T(8,128)} copy(f32[1,16,16,16,512]{4,3,2,1,0:T(8,128)S(1)} %get-tuple-element.3) | data formatting | bytes 16777216 | tf_op jit(solution)/shard_map/convert_element_type | solution.py:41
  123.5 24.3 %all-gather.3.cloned.1.call-done = f32[16,256,512]{2,1,0:T(8,128)} async-done(((f32[16,16,512]{2,1,0:T(8,128)}), f32[16,256,512]{2,1,0:T(8,128)}) %all-gather.3.cloned.1.call-update) | async-done | bytes 8388624 | tf_op jit(solution)/shard_map/all_gather | solution.py:37
  147.9 11.4 %mul.124 = f32[16,256,512]{2,1,0:T(8,128)} multiply(f32[16,256,512]{2,1,0:T(8,128)} %bitcast.77, f32[16,256,512]{2,1,0:T(8,128)} %all-gather.3.cloned.1.call-done) | non-fusion elementwise | flops 2097152 | bytes 25165824 | tf_op jit(solution)/shard_map/mul | solution.py:42
  159.3 17.2 %fusion.5 = f32[16,256,512]{2,0,1:T(8,128)S(1)} fusion(f32[16,256,512]{2,1,0:T(8,128)} %mul.124, f32[16,16]{1,0:T(8,128)S(1)} %copy-done.1, f32[16]{0:T(128)S(1)} %compare_convert_fusion), kind=kOutput, calls=%fused_computation.7 | convolution fusion | flops 402653440 | bytes 16778304 | tf_op jit(solution)/shard_map/zk,mzyx->mkyx/dot_general | solution.py:43
  176.6 16.3 %fusion.1 = f32[16,256,256]{1,2,0:T(8,128)} fusion(f32[16,256,512]{2,0,1:T(8,128)S(1)} %fusion.5, f32[256]{0:T(256)S(1)} %compare_select_fusion.3, f32[512]{0:T(512)S(1)} %add_multiply_fusion), kind=kOutput, calls=%fused_computation.2 | convolution fusion | flops 6442844160 | bytes 12585984 | tf_op jit(solution)/shard_map/mkyx,xp->mkyp/dot_general | solution.py:44
  192.9 2.2 all-gather.5.cloned.1.call-done
  195.1 6.9 fusion.8
  202.1 6.0 convolution_bitcast_fusion
  208.1 5.5 copy.25
  213.5 12.5 %fusion.14 = f32[16,256,512]{2,0,1:T(8,128)S(1)} fusion(f32[16,256,256]{2,0,1:T(8,128)} %copy.25, f32[256]{0:T(256)S(1)} %compare_select_fusion.3, f32[512]{0:T(512)S(1)} %add_multiply_fusion), kind=kOutput, calls=%fused_computation.19 | convolution fusion | flops 6442844160 | bytes 12585984 | tf_op jit(solution)/shard_map/mkyp,xp->mkyx/dot_general | solution.py:53
  226.0 12.4 %fusion = f32[1,16,256,512]{3,1,2,0:T(8,128)} fusion(f32[1,16,256,512]{3,1,2,0:T(8,128)} %bitcast.78, f32[16,256,512]{2,0,1:T(8,128)S(1)} %fusion.14, f32[16,16]{1,0:T(8,128)S(1)} %copy-done.1, f32[16]{0:T(128)S(1)} %compare_convert_fusion), kind=kOutput, calls=%fused_computation.1 | convolution fusion | flops 406847744 | bytes 25166912 | tf_op jit(solution)/shard_map/zk,mkyx->mzyx/dot_general | solution.py:54
  238.4 10.8 %reshape.99 = f32[8,2,16,16,512]{4,1,0,3,2:T(2,128)} reshape(f32[1,16,256,512]{3,1,2,0:T(8,128)} %fusion) | data formatting | bytes 16777216 | tf_op jit(solution)/shard_map/reshape | solution.py:58
  249.2 11.5 %copy.26 = f32[8,16,2,16,512]{4,3,2,1,0:T(8,128)} copy(f32[8,16,2,16,512]{4,2,0,3,1:T(2,128)} %bitcast.80) | data formatting | bytes 16777216 | tf_op jit(solution)/shard_map/transpose | solution.py:59
  260.7 1.2 copy.27
  262.0 34.7 %all_to_all.27 = f32[1,16,128,256]{2,1,0,3:T(8,128)S(1)} all-to-all(f32[1,16,128,256]{2,1,0,3:T(8,128)S(1)} %copy.27), channel_id=1, replica_groups=mesh['mem'=8,'grid'=16] {'grid'}, dimensions={3} | all-to-all | bytes 4194304 | tf_op jit(solution)/shard_map/all_to_all | solution.py:56
  296.6 2.0 copy.42
  298.6 633.6 %reduce-scatter.2.cloned.1.call-done = f32[1,2,16,512]{3,2,1,0:T(8,128)} async-done(((f32[128,2,16,512]{3,2,1,0:T(8,128)}), f32[1,2,16,512]{3,2,1,0:T(8,128)}) %reduce-scatter.2.cloned.1.call-update) | async-done | bytes 65552 | tf_op jit(solution)/shard_map/reduce_scatter | solution.py:62
  (15 shorter events, 0.1 us)
Async XLA Ops:
  7.2 140.7 %all-gather.3.cloned.1.call-start = ((), (), s32[]{:S(2)}) async-start(), calls=%async_computation.3 | async-start | bytes 8912896 | tf_op jit(solution)/shard_map/all_gather | solution.py:37
  39.7 66.1 %all-to-all-start = ((bf16[16,16,16,512]{3,2,1,0:T(8,128)(2,1)}), bf16[16,16,16,512]{3,2,1,0:T(8,128)(2,1)}, u32[]{:S(2)}, u32[]{:S(2)}) async-start(bf16[16,16,16,512]{3,2,1,0:T(8,128)(2,1)} %param.7), calls=%async_computation | async-start | bytes 8388608 | tf_op jit(solution)/shard_map/all_to_all | solution.py:40
  47.8 147.3 %all-gather.5.cloned.1.call-start = ((), (), s32[]{:S(2)}) async-start(), calls=%async_computation.4 | async-start | bytes 2228224 | tf_op jit(solution)/shard_map/all_gather | solution.py:38
  48.6 883.7 %reduce-scatter.2.cloned.1.call-start = ((), (), s32[]{:S(2)}) async-start(), calls=%async_computation.5 | async-start | bytes 8454144 | tf_op jit(solution)/shard_map/reduce_scatter | solution.py:62
  147.9 11.4 %copy-start.1 = (f32[16,16]{1,0:T(8,128)S(1)}, f32[16,16]{1,0:T(8,128)}, u32[]{:S(2)}) copy-start(f32[16,16]{1,0:T(8,128)} %param.8) | copy-start | bytes 3076
  176.6 18.6 %copy-start.2 = (s32[16]{0:T(128)S(1)}, s32[16]{0:T(128)}, u32[]{:S(2)}) copy-start(s32[16]{0:T(128)} %param.10) | copy-start | bytes 196
  195.1 6.9 copy-start
Sparse Core Ops, SparseCore 0:
  39.9 107.9 all-gather.2
  150.2 44.8 all-gather.4
  260.9 671.3 reduce-scatter.1
where the time goes:
time: 948 us; the launch traced here: 939 us
  waiting for transfers between devices  717 us (76%)
  matrix products  71.3 us (8%)
  blocking collectives  67.2 us (7%)
  local copies, waits for them, and re-layouts  41 us (4%)
  other arithmetic  19.1 us (2%)
  between operations  14.9 us (2%)
    reduce_scatter x1, waiting for transfers between devices, local(): lax.psum_scatter(blocks, ('mem', 'grid'), scatter_dimension=0, tiled=True)  634 us
    all_to_all x1, waiting for transfers between devices, local(): lax.all_to_all(members, 'grid', split_axis=0, concat_axis=2, tiled=True)  56.5 us
    all_to_all x1, blocking collectives, local(): lax.all_to_all(local_control, 'grid', split_axis=3, concat_axis=0, tiled=...  34.7 us
    all_gather x1, blocking collectives, local(): levels = lax.all_gather(gradient, 'mem', axis=0, tiled=True)  32.5 us
    all_gather x1, waiting for transfers between devices, local(): whole_grad = lax.all_gather(levels, 'grid', axis=1, tiled=True)  24.3 us
  transfers between devices with their start and end apart: 4, of which 4 were waited for; matrix products, arithmetic and copies ran while one was open for 7% of the time, Pallas kernels for 0%

commit v1 on v0

v1 whole, which is shorter than its diff:
```python
import functools
import math

import jax
import jax.numpy as jnp
import numpy as np
from jax import lax
from jax.experimental import pallas as pl
from jax.experimental.pallas import tpu as pltpu
from jax.sharding import PartitionSpec as P

F32 = jnp.float32
BF16 = jnp.bfloat16
LANES = 128
CHUNKS = 1
VMEM_LIMIT = 48 * 1024 * 1024


def cosine_table(length, retain_count):
    cells = np.arange(length, dtype=np.float64)
    waves = np.arange(retain_count, dtype=np.float64)
    factor = np.where(waves == 0.0, math.sqrt(1.0 / length), math.sqrt(2.0 / length))
    return np.cos(math.pi * (cells[:, None] + 0.5) * waves[None, :] / length) * factor[None, :]


def table_parts(table):
    high = table.astype(jnp.bfloat16)
    low = (table - high.astype(np.float64)).astype(jnp.bfloat16)
    return high, low


def parts(value):
    high = value.astype(BF16)
    return high, (value - high.astype(F32)).astype(BF16)


def dot3(a, b, dims):
    dot = functools.partial(
        lax.dot_general, dimension_numbers=(dims, ((), ())), preferred_element_type=F32
    )
    return dot(a[0], b[0]) + (dot(a[0], b[1]) + dot(a[1], b[0]))


def regroup(pieces, width):
    pieces = list(pieces)
    count = len(pieces)
    group = lax.broadcasted_iota(jnp.int32, pieces[0].shape, 1) // width
    step = 1
    while step < count:
        upper = (group & step) != 0
        for a in range(count):
            if a & step:
                continue
            low, high = pieces[a], pieces[a | step]
            pieces[a] = jnp.where(upper, pltpu.roll(high, step * width, 1), low)
            pieces[a | step] = jnp.where(
                upper, high, pltpu.roll(low, LANES - step * width, 1)
            )
        step *= 2
    return pieces


def encode(tile):
    peak = jnp.maximum(jnp.max(jnp.abs(tile), axis=0, keepdims=True), 2.0**-80)
    power = jnp.ceil(jnp.log2(peak)) - 15.0
    code = jnp.clip(jnp.round(tile * jnp.exp2(-power)), -32767.0, 32767.0)
    return code.astype(jnp.int32).astype(jnp.int16), power


def spread(basis, rows, transposed):
    count = basis.shape[0]
    size = count * rows
    one = (
        lax.broadcasted_iota(jnp.int32, (size, count), 0) // rows
        == lax.broadcasted_iota(jnp.int32, (size, count), 1)
    ).astype(BF16)
    same = (
        lax.broadcasted_iota(jnp.int32, (size, size), 0) % rows
        == lax.broadcasted_iota(jnp.int32, (size, size), 1) % rows
    )
    out = []
    for part in parts(basis):
        inner = (((1,), (1 if transposed else 0,)), ((), ()))
        left = lax.dot_general(one, part, inner, preferred_element_type=F32).astype(BF16)
        whole = lax.dot_general(
            left, one, (((1,), (1,)), ((), ())), preferred_element_type=F32
        )
        out.append(jnp.where(same, whole, 0.0).astype(BF16))
    return out


def masked_basis(basis_ref, mode_count_ref):
    basis = basis_ref[...]
    mode = lax.broadcasted_iota(jnp.int32, basis.shape, 1)
    return jnp.where(mode < mode_count_ref[0], basis, 0.0)


def tail_tiles(count):
    return -(-2 * count // 16)


def store_powers(power_ref, message_ref, count):
    tiles = tail_tiles(count)
    for j in range(16):
        for t in range(tiles):
            message_ref[j, 2 * count + t] = (
                power_ref[j, 16 * t : 16 * t + 16, :].astype(jnp.int32).astype(jnp.int16)
            )


def load_scales(message_ref, scale_ref, count):
    tiles = tail_tiles(count)
    for j in range(16):
        for t in range(tiles):
            power = message_ref[j, 2 * count + t].astype(jnp.int32).astype(F32)
            scale_ref[j, 16 * t : 16 * t + 16, :] = jnp.exp2(power)


def forward_rows(
    count, mode_count_ref, members_ref, grad_ref, basis_ref, xhi_ref, xlo_ref,
    message_ref, bhi_ref, blo_ref, power_ref,
):
    step = pl.program_id(0)

    @pl.when(step == 0)
    def _():
        hi, lo = spread(masked_basis(basis_ref, mode_count_ref), 16, True)
        bhi_ref[...] = hi
        blo_ref[...] = lo
        power_ref[...] = jnp.zeros_like(power_ref)

    product = (members_ref[0].astype(F32) * grad_ref[...]).reshape(256, 512)
    spectrum = dot3(parts(product), (xhi_ref[...], xlo_ref[...]), ((1,), (0,)))
    modes = dot3((bhi_ref[...], blo_ref[...]), parts(spectrum), ((1,), (0,)))
    for kh in range(2):
        for jh in range(2):
            pieces = [
                modes[(kh * 8 + k) * 16 : (kh * 8 + k + 1) * 16, jh * LANES : (jh + 1) * LANES]
                for k in range(8)
            ]
            for j, piece in enumerate(regroup(pieces, 16)):
                code, power = encode(piece)
                message_ref[jh * 8 + j, 2 * step + kh] = code
                power_ref[jh * 8 + j, pl.ds(2 * step + kh, 1), :] = power

    @pl.when(step == count - 1)
    def _():
        store_powers(power_ref, message_ref, count)


def spectral(
    count, member_scale, retained_ref, offset_ref, message_ref, weight_ref, yhi_ref, ylo_ref,
    control_ref, back_ref, filter_ref, scale_ref, power_ref,
):
    step = pl.program_id(0)

    @pl.when(step == 0)
    def _():
        load_scales(message_ref, scale_ref, count)
        power_ref[...] = jnp.zeros_like(power_ref)
        wave = (
            lax.broadcasted_iota(jnp.int32, (16, LANES), 0)
            + lax.broadcasted_iota(jnp.int32, (16, LANES), 1)
            + offset_ref[0]
        )
        for k in range(16):
            filter_ref[16 * k : 16 * k + 16, :] = jnp.where(
                wave < retained_ref[k], weight_ref[k], 0.0
            )

    y_table = (yhi_ref[...], ylo_ref[...])
    for kh in range(2):
        rows = slice(kh * 128, kh * 128 + 128)
        code = message_ref[:, 2 * step + kh].astype(jnp.int32).astype(F32)
        scale = scale_ref[:, pl.ds(2 * step + kh, 1), :]
        lines = (code * scale).reshape(256, LANES)
        band = filter_ref[rows, :]
        control = dot3(parts(lines), y_table, ((0,), (0,))) * (band * member_scale)
        control_ref[0, kh * 8 : kh * 8 + 8] = control.reshape(8, 16, LANES)
        back = dot3(y_table, parts(control * band), ((1,), (1,)))
        for i in range(16):
            code, power = encode(back[16 * i : 16 * i + 16, :])
            back_ref[i, 2 * step + kh] = code
            power_ref[i, pl.ds(2 * step + kh, 1), :] = power

    @pl.when(step == count - 1)
    def _():
        store_powers(power_ref, back_ref, count)


def backward_rows(
    count, member_scale, first, mode_count_ref, members_ref, back_ref, basis_ref, xhi_ref, xlo_ref,
    *rest,
):
    if first:
        total_ref, bhi_ref, blo_ref, scale_ref, rows_ref = rest
    else:
        before_ref, total_ref, bhi_ref, blo_ref, scale_ref, rows_ref = rest
    step = pl.program_id(0)

    @pl.when(step == 0)
    def _():
        hi, lo = spread(masked_basis(basis_ref, mode_count_ref) * member_scale, 16, False)
        bhi_ref[...] = hi
        blo_ref[...] = lo
        load_scales(back_ref, scale_ref, count)
        if first:
            total_ref[...] = jnp.zeros_like(total_ref)
        else:
            total_ref[...] = before_ref[...]

    for kh in range(2):
        for jh in range(2):
            pieces = []
            for j in range(8):
                code = back_ref[jh * 8 + j, 2 * step + kh].astype(jnp.int32).astype(F32)
                pieces.append(code * scale_ref[jh * 8 + j, pl.ds(2 * step + kh, 1), :])
            for k, piece in enumerate(regroup(pieces, 16)):
                row = (kh * 8 + k) * 16
                rows_ref[row : row + 16, jh * LANES : (jh + 1) * LANES] = piece
    levels = dot3((bhi_ref[...], blo_ref[...]), parts(rows_ref[...]), ((1,), (0,)))
    vertical = dot3(parts(levels), (xhi_ref[...], xlo_ref[...]), ((1,), (1,)))
    total_ref[...] += members_ref[0].astype(F32) * vertical.reshape(16, 16, 512)


def whole(shape):
    return pl.BlockSpec(shape, lambda m: (0,) * len(shape))


SMEM = pl.BlockSpec(memory_space=pltpu.SMEM)


def params():
    return pltpu.CompilerParams(
        dimension_semantics=("arbitrary",), vmem_limit_bytes=VMEM_LIMIT
    )


def local(gradient, members, eof_basis, spectral_weight, retained, mode_count):
    group_count = lax.axis_size("mem")
    held = members.shape[0]
    member_total = held * group_count
    member_scale = 1.0 / math.sqrt(member_total - 1)
    xhi, xlo = (jnp.asarray(t) for t in table_parts(cosine_table(512, 256)))
    yhi, ylo = (jnp.asarray(t) for t in table_parts(cosine_table(256, 128)))
    share = gradient.shape[0]
    spreads = jnp.broadcast_to(gradient[None], (group_count,) + gradient.shape)
    levels = lax.all_to_all(spreads, "mem", 0, 0, tiled=True).reshape(16, 16, 512)
    offset = (lax.axis_index("grid") * 16).astype(jnp.int32).reshape(1)
    weight = spectral_weight.transpose(0, 2, 1)

    count = held // CHUNKS
    tiles = 2 * count + tail_tiles(count)
    tail = 16 * tail_tiles(count)
    message_shape = (16, tiles, 16, LANES)
    message_type = jax.ShapeDtypeStruct(message_shape, jnp.int16)
    basis_scratch = pltpu.VMEM((256, 256), BF16)
    power_scratch = pltpu.VMEM((16, tail, LANES), F32)

    def member_block(chunk):
        return pl.BlockSpec((1, 16, 16, 512), lambda m: (m + chunk * count, 0, 0, 0))

    controls = []
    total = None
    messages = []
    for chunk in range(CHUNKS):
        message = pl.pallas_call(
            functools.partial(forward_rows, count),
            grid=(count,),
            in_specs=[
                SMEM, member_block(chunk), whole((16, 16, 512)), whole((16, 16)),
                whole((512, 256)), whole((512, 256)),
            ],
            out_specs=whole(message_shape),
            out_shape=message_type,
            scratch_shapes=[basis_scratch, basis_scratch, power_scratch],
            compiler_params=params(),
            name="forward_rows",
        )(mode_count, members, levels, eof_basis, xhi, xlo)
        messages.append(lax.all_to_all(message, "grid", 0, 0, tiled=True))
    backs = []
    for chunk in range(CHUNKS):
        control, back = pl.pallas_call(
            functools.partial(spectral, count, member_scale),
            grid=(count,),
            in_specs=[
                SMEM, SMEM, whole(message_shape), whole((16, 16, 128)),
                whole((256, 128)), whole((256, 128)),
            ],
            out_specs=[
                pl.BlockSpec((1, 16, 16, 128), lambda m: (m, 0, 0, 0)), whole(message_shape)
            ],
            out_shape=[jax.ShapeDtypeStruct((count, 16, 16, 128), F32), message_type],
            scratch_shapes=[pltpu.VMEM((256, 128), F32), power_scratch, power_scratch],
            compiler_params=params(),
            name="spectral",
        )(retained, offset, messages[chunk], weight, yhi, ylo)
        controls.append(control)
        backs.append(lax.all_to_all(back, "grid", 0, 0, tiled=True))
    for chunk in range(CHUNKS):
        first = chunk == 0
        total = pl.pallas_call(
            functools.partial(backward_rows, count, member_scale, first),
            grid=(count,),
            in_specs=[
                SMEM, member_block(chunk), whole(message_shape), whole((16, 16)),
                whole((512, 256)), whole((512, 256)),
            ]
            + ([] if first else [whole((16, 16, 512))]),
            out_specs=whole((16, 16, 512)),
            out_shape=jax.ShapeDtypeStruct((16, 16, 512), F32),
            scratch_shapes=[
                basis_scratch, basis_scratch, power_scratch, pltpu.VMEM((256, 256), F32)
            ],
            compiler_params=params(),
            name="backward_rows",
        )(mode_count, members, backs[chunk], eof_basis, xhi, xlo, *([] if first else [total]))
    blocks = total.reshape(group_count, share, 16, 512)
    increment = jnp.sum(lax.all_to_all(blocks, "mem", 0, 0, tiled=True), axis=0)
    control = controls[0] if CHUNKS == 1 else jnp.concatenate(controls, 0)
    return (increment, control.transpose(0, 1, 3, 2))


def solution(mesh):
    return jax.shard_map(
        local,
        mesh=mesh,
        in_specs=(
            P("mem", "grid", None),
            P("mem", None, "grid", None),
            P(),
            P(None, None, "grid"),
            P(),
            P(),
        ),
        out_specs=(P("mem", "grid", None), P("mem", None, None, "grid")),
        check_vma=False,
    )
```

time: 948 us -> 158 us (0.17)
  waiting for transfers between devices: 717 us -> 40.1 us
  matrix products: 71.3 us -> 0 us
  Pallas kernels: 0 us -> 50.1 us
  local copies, waits for them, and re-layouts: 41 us -> 5.68 us
  blocking collectives: 67.2 us -> 46.6 us
  other arithmetic: 19.1 us -> 0.67 us
  between operations: 14.9 us -> 1.35 us
    reduce_scatter x1 -> x0, waiting for transfers between devices: 634 us -> none  [local(): lax.psum_scatter(blocks, ('mem', 'grid'), scatter_dimension=0, tiled=True)]
    dot_general x6 -> x0, matrix products: 71.3 us -> none  [the longest x1 17.2 us: local(): projected = jnp.einsum('zk,mzyx->mkyx', basis, product, precision=high)]
    pallas_call x0 -> x3, Pallas kernels: none -> 50.1 us  [the longest x1 18.4 us: local(): pl.pallas_call(functools.partial(forward_rows, count), grid=(count,), in_...]
    all_gather x1 -> x0, blocking collectives: 32.5 us -> none  [local(): levels = lax.all_gather(gradient, 'mem', axis=0, tiled=True)]
    all_gather x2 -> x0, waiting for transfers between devices: 26.6 us -> none  [the longest x1 24.3 us: local(): whole_grad = lax.all_gather(levels, 'grid', axis=1, tiled=True)]
    all_to_all x1 -> x2, waiting for transfers between devices: 56.5 us -> 40.1 us  [the longest x1 30.7 us: local(): messages.append(lax.all_to_all(message, 'grid', 0, 0, tiled=True))]
    all_to_all x1 -> x2, blocking collectives: 34.7 us -> 46.6 us  [the longest x1 33.8 us: local(): backs.append(lax.all_to_all(back, 'grid', 0, 0, tiled=True))]
    transpose x1 -> x0, local copies, waits for them, and re-layouts: 11.5 us -> none  [local(): blocks.transpose(0, 2, 1, 3, 4)]
  transfers between devices with their start and end apart: 4 -> 2, of which waited for: 4 -> 2; matrix products, arithmetic and copies ran while one was open for 7% -> 0% of each run, Pallas kernels for 0% -> 0%
where the time goes in v1:
time: 158 us
  Pallas kernels  50.1 us (32%)
  blocking collectives  46.6 us (29%)
  waiting for transfers between devices  40.1 us (25%)
  starting transfers between devices  13.2 us (8%)
  local copies, waits for them, and re-layouts  5.68 us (4%)
    all_to_all x1, blocking collectives, local(): backs.append(lax.all_to_all(back, 'grid', 0, 0, tiled=True))  33.8 us
    all_to_all x1, waiting for transfers between devices, local(): messages.append(lax.all_to_all(message, 'grid', 0, 0, tiled=True))  30.7 us
    pallas_call x1, Pallas kernels, local(): pl.pallas_call(functools.partial(forward_rows, count), grid=(count,), in_...  18.4 us
    pallas_call x1, Pallas kernels, local(): pl.pallas_call(functools.partial(backward_rows, count, member_scale, firs...  17.1 us
    pallas_call x1, Pallas kernels, local(): pl.pallas_call(functools.partial(spectral, count, member_scale), grid=(co...  14.5 us
    all_to_all x1, blocking collectives, local(): increment = jnp.sum(lax.all_to_all(blocks, 'mem', 0, 0, tiled=True), axis=0)  12.8 us
    all_to_all x1, waiting for transfers between devices, local(): lax.all_to_all(spreads, 'mem', 0, 0, tiled=True).reshape(16, 16, 512)  9.43 us
    all_to_all x1, starting transfers between devices, local(): messages.append(lax.all_to_all(message, 'grid', 0, 0, tiled=True))  7.72 us
  transfers between devices with their start and end apart: 2, of which 2 were waited for; matrix products, arithmetic and copies ran while one was open for 0% of the time, Pallas kernels for 0%

profile of v1, /device:TPU:0, one launch (start us, length us, event | category | flops | bytes accessed | tf_op | source)
XLA Modules:
  0.0 157.7 jit_solution(5218694348981490023)
XLA Ops:
  0.6 1.7 %broadcast_in_dim.2 = f32[8,2,16,512]{3,2,1,0:T(8,128)} broadcast(f32[2,16,512]{2,1,0:T(8,128)} %param.10), dimensions={1,2,3} | broadcast | bytes 589824 | tf_op jit(solution)/shard_map/broadcast_in_dim | solution.py:247
  2.3 5.5 %all-to-all-start = ((f32[8,2,16,512]{3,2,1,0:T(8,128)}), f32[8,2,16,512]{3,2,1,0:T(8,128)S(1)}, u32[]{:S(2)}, u32[]{:S(2)}) async-start(f32[8,2,16,512]{3,2,1,0:T(8,128)} %broadcast_in_dim.2), calls=%async_computation | async-start | bytes 1048576 | tf_op jit(solution)/shard_map/all_to_all | solution.py:248
  8.5 9.4 %all-to-all-done = f32[8,2,16,512]{3,2,1,0:T(8,128)S(1)} async-done(((f32[8,2,16,512]{3,2,1,0:T(8,128)}), f32[8,2,16,512]{3,2,1,0:T(8,128)S(1)}, u32[]{:S(2)}, u32[]{:S(2)}) %all-to-all-start) | async-done | bytes 524320 | tf_op jit(solution)/shard_map/all_to_all | solution.py:248
  17.9 0.0 copy-start.1
  17.9 0.9 copy-done.1
  18.8 0.9 copy-done.3
  19.8 0.7 copy-done.8
  20.5 18.4 %forward_rows.1 = s16[16,34,16,128]{3,2,1,0:T(8,128)(2,1)S(1)} custom-call(s32[1]{0:T(128)S(6)} %copy.12.mode_count_ref, bf16[16,16,16,512]{3,2,1,0:T(8,128)(2,1)} %members_ref.3, f32[16,16,512]{2,1,0:T(8,128)S(1)} %bitcast.5, f32[16,16]{1,0:T(8,128)S(1)} %copy-done.8, bf16[512,256]{1,0:T(8,128)(2,1)S(1)} %copy-done.3, bf16[512,256]{1,0:T(8,128)(2,1)S(1)} %copy-done.1), custom_call_target="tpu_custom_call" | custom-call | tf_op jit(solution)/shard_map/forward_rows/pallas_call | solution.py:267
  38.9 0.0 copy-start
  38.9 1.4 copy-done
  40.3 7.7 %all-to-all-start.1 = ((s16[16,34,16,128]{3,2,1,0:T(8,128)(2,1)}), s16[16,34,16,128]{3,2,1,0:T(8,128)(2,1)S(1)}, u32[]{:S(2)}, u32[]{:S(2)}) async-start(s16[16,34,16,128]{3,2,1,0:T(8,128)(2,1)} %copy-done), calls=%async_computation.1 | async-start | bytes 4456448 | tf_op jit(solution)/shard_map/all_to_all | solution.py:280
  48.0 30.7 %all-to-all-done.1.message_ref = s16[16,34,16,128]{3,2,1,0:T(8,128)(2,1)S(1)} async-done(((s16[16,34,16,128]{3,2,1,0:T(8,128)(2,1)}), s16[16,34,16,128]{3,2,1,0:T(8,128)(2,1)S(1)}, u32[]{:S(2)}, u32[]{:S(2)}) %all-to-all-start.1) | async-done | bytes 2228256 | tf_op jit(solution)/shard_map/all_to_all | solution.py:280
  78.7 0.0 copy-done.5
  78.8 0.0 copy-done.6
  78.8 0.0 copy-done.7
  78.8 0.0 copy-done.10
  78.8 14.5 %spectral.1 = (f32[16,16,16,128]{3,2,1,0:T(8,128)}, s16[16,34,16,128]{3,2,1,0:T(8,128)(2,1)S(1)}) custom-call(s32[16]{0:T(128)S(1)} %copy-done.10, s32[1]{0:T(128)} %bitcast.offset_ref, s16[16,34,16,128]{3,2,1,0:T(8,128)(2,1)S(1)} %all-to-all-done.1.message_ref, f32[16,16,128]{2,1,0:T(8,128)S(1)} %bitcast.7, bf16[256,128]{1,0:T(8,128)(2,1)S(1)} %copy-done.7, ...), custom_call_target="tpu_custom_call" | custom-call | tf_op jit(solution)/shard_map/spectral/pallas_call | solution.py:283
  93.3 33.8 %all_to_all.20.back_ref = s16[16,34,16,128]{3,2,1,0:T(8,128)(2,1)S(1)} all-to-all(s16[16,34,16,128]{3,2,1,0:T(8,128)(2,1)S(1)} %get-tuple-element.4), channel_id=1, replica_groups=mesh['mem'=8,'grid'=16] {'grid'}, dimensions={0} | all-to-all | bytes 4456448 | tf_op jit(solution)/shard_map/all_to_all | solution.py:299
  127.1 0.0 copy-done.2
  127.1 0.0 copy-done.4
  127.1 0.0 copy-done.9
  127.1 17.1 %backward_rows.1 = f32[16,16,512]{2,1,0:T(8,128)S(1)} custom-call(s32[1]{0:T(128)S(6)} %copy.12.mode_count_ref, bf16[16,16,16,512]{3,2,1,0:T(8,128)(2,1)} %members_ref.3, s16[16,34,16,128]{3,2,1,0:T(8,128)(2,1)S(1)} %all_to_all.20.back_ref, f32[16,16]{1,0:T(8,128)S(1)} %copy-done.9, bf16[512,256]{1,0:T(8,128)(2,1)S(1)} %copy-done.4, ...), custom_call_target="tpu_custom_call" | custom-call | tf_op jit(solution)/shard_map/backward_rows/pallas_call | solution.py:302
  144.2 12.8 %all_to_all.21 = f32[8,2,16,512]{3,2,1,0:T(8,128)S(1)} all-to-all(f32[8,2,16,512]{3,2,1,0:T(8,128)S(1)} %bitcast.6), channel_id=1, replica_groups=mesh['mem'=8,'grid'=16] {'mem'}, dimensions={0} | all-to-all | bytes 1048576 | tf_op jit(solution)/shard_map/all_to_all | solution.py:319
  157.0 0.7 reduce_sum.9
  (9 shorter events, 0.0 us)
Async XLA Ops:
  2.3 15.6 %all-to-all-start = ((f32[8,2,16,512]{3,2,1,0:T(8,128)}), f32[8,2,16,512]{3,2,1,0:T(8,128)S(1)}, u32[]{:S(2)}, u32[]{:S(2)}) async-start(f32[8,2,16,512]{3,2,1,0:T(8,128)} %broadcast_in_dim.2), calls=%async_computation | async-start | bytes 1048576 | tf_op jit(solution)/shard_map/all_to_all | solution.py:248
  17.9 1.0 copy-start.1
  18.8 0.9 copy-start.3
  19.8 0.7 copy-start.8
  38.9 1.4 copy-start
  40.3 38.5 %copy-start.5 = (f32[16,128,16]{1,2,0:T(8,128)S(1)}, f32[16,128,16]{1,2,0:T(8,128)}, u32[]{:S(2)}) copy-start(f32[16,128,16]{1,2,0:T(8,128)} %param.13) | copy-start | bytes 393220
  40.3 38.5 %copy-start.6 = (bf16[256,128]{1,0:T(8,128)(2,1)S(1)}, bf16[256,128]{1,0:T(8,128)(2,1)}, u32[]{:S(2)}) copy-start(bf16[256,128]{1,0:T(8,128)(2,1)} %constant.19.clone.ylo_ref) | copy-start | bytes 196612
  40.3 38.5 %copy-start.7 = (bf16[256,128]{1,0:T(8,128)(2,1)S(1)}, bf16[256,128]{1,0:T(8,128)(2,1)}, u32[]{:S(2)}) copy-start(bf16[256,128]{1,0:T(8,128)(2,1)} %constant.18.clone.yhi_ref) | copy-start | bytes 196612
  40.3 38.5 %copy-start.10 = (s32[16]{0:T(128)S(1)}, s32[16]{0:T(128)}, u32[]{:S(2)}) copy-start(s32[16]{0:T(128)} %retained_ref.1) | copy-start | bytes 196
  40.3 38.4 %all-to-all-start.1 = ((s16[16,34,16,128]{3,2,1,0:T(8,128)(2,1)}), s16[16,34,16,128]{3,2,1,0:T(8,128)(2,1)S(1)}, u32[]{:S(2)}, u32[]{:S(2)}) async-start(s16[16,34,16,128]{3,2,1,0:T(8,128)(2,1)} %copy-done), calls=%async_computation.1 | async-start | bytes 4456448 | tf_op jit(solution)/shard_map/all_to_all | solution.py:280
  93.3 33.8 %copy-start.2 = (bf16[512,256]{1,0:T(8,128)(2,1)S(1)}, bf16[512,256]{1,0:T(8,128)(2,1)}, u32[]{:S(2)}) copy-start(bf16[512,256]{1,0:T(8,128)(2,1)} %constant.17.clone.xlo_ref) | copy-start | bytes 786436
  93.3 33.8 %copy-start.4 = (bf16[512,256]{1,0:T(8,128)(2,1)S(1)}, bf16[512,256]{1,0:T(8,128)(2,1)}, u32[]{:S(2)}) copy-start(bf16[512,256]{1,0:T(8,128)(2,1)} %constant.16.clone.xhi_ref) | copy-start | bytes 786436
  93.3 33.8 %copy-start.9 = (f32[16,16]{1,0:T(8,128)S(1)}, f32[16,16]{1,0:T(8,128)}, u32[]{:S(2)}) copy-start(f32[16,16]{1,0:T(8,128)} %basis_ref.3) | copy-start | bytes 3076

commit v2 on v0

v2 whole, which is shorter than its diff:
```python
import functools
import math

import jax
import jax.numpy as jnp
import numpy as np
from jax import lax
from jax.experimental import pallas as pl
from jax.experimental.pallas import tpu as pltpu
from jax.sharding import PartitionSpec as P

F32 = jnp.float32
BF16 = jnp.bfloat16
LANES = 128
CHUNKS = 1
GROUP = 4
VMEM_LIMIT = 48 * 1024 * 1024


def cosine_table(length, retain_count):
    cells = np.arange(length, dtype=np.float64)
    waves = np.arange(retain_count, dtype=np.float64)
    factor = np.where(waves == 0.0, math.sqrt(1.0 / length), math.sqrt(2.0 / length))
    return np.cos(math.pi * (cells[:, None] + 0.5) * waves[None, :] / length) * factor[None, :]


def table_parts(table):
    high = table.astype(jnp.bfloat16)
    low = (table - high.astype(np.float64)).astype(jnp.bfloat16)
    return high, low


def parts(value):
    high = value.astype(BF16)
    return high, (value - high.astype(F32)).astype(BF16)


def dot(a, b):
    return lax.dot_general(a, b, (((1,), (0,)), ((), ())), preferred_element_type=F32)


def left_parts(value):
    high, low = parts(value)
    return jnp.concatenate([high, low, high], axis=1)


def right_parts(value):
    high, low = parts(value)
    return jnp.concatenate([high, high, low], axis=0)


def regroup(pieces, width):
    pieces = list(pieces)
    count = len(pieces)
    group = lax.broadcasted_iota(jnp.int32, pieces[0].shape, 1) // width
    step = 1
    while step < count:
        upper = (group & step) != 0
        for a in range(count):
            if a & step:
                continue
            low, high = pieces[a], pieces[a | step]
            pieces[a] = jnp.where(upper, pltpu.roll(high, step * width, 1), low)
            pieces[a | step] = jnp.where(
                upper, high, pltpu.roll(low, LANES - step * width, 1)
            )
        step *= 2
    return pieces


def peak(tile):
    return jnp.max(jnp.abs(tile), axis=0, keepdims=True)


def power_of(peaks):
    return jnp.ceil(jnp.log2(jnp.maximum(peaks, 2.0**-80) * (1.0 + 2.0**-12))) - 15.0


def to_code(scaled):
    return jnp.round(scaled).astype(jnp.int32).astype(jnp.int16)


def from_code(code):
    return code.astype(jnp.int32).astype(F32)


def pick(size, count):
    row = lax.broadcasted_iota(jnp.int32, (size, count), 0) // 16
    return (row == lax.broadcasted_iota(jnp.int32, (size, count), 1)).astype(BF16)


def spread(basis, rows, columns):
    same = (
        lax.broadcasted_iota(jnp.int32, (rows, columns), 0) % 16
        == lax.broadcasted_iota(jnp.int32, (rows, columns), 1) % 16
    )
    out = []
    for part in parts(basis):
        left = dot(pick(rows, 16), part).astype(BF16)
        full = lax.dot_general(
            left, pick(columns, 16), (((1,), (1,)), ((), ())), preferred_element_type=F32
        )
        out.append(jnp.where(same, full, 0.0).astype(BF16))
    return jnp.concatenate([out[0], out[1], out[0]], axis=1)


def masked_basis(basis_ref, mode_count_ref, mode_axis):
    basis = basis_ref[...]
    mode = lax.broadcasted_iota(jnp.int32, basis.shape, mode_axis)
    return jnp.where(mode < mode_count_ref[0], basis, 0.0)


def store_powers(power_ref, message_ref, first_tile):
    groups = power_ref.shape[1]
    for j in range(16):
        for t in range(groups // 2):
            pair = [power_ref[j, 2 * t], power_ref[j, 2 * t + 1]]
            message_ref[j, first_tile + t] = to_code(jnp.concatenate(pair, axis=0))


def forward_rows(
    tiles, modes, mode_count_ref, members_ref, grad_ref, basis_ref, table_ref,
    message_ref, spread_ref, power_ref,
):
    step = pl.program_id(0)
    steps = pl.num_programs(0)

    @pl.when(step == 0)
    def _():
        spread_ref[...] = spread(masked_basis(basis_ref, mode_count_ref, 0), modes * 16, 256)
        power_ref[...] = jnp.zeros_like(power_ref)

    product = members_ref[...].astype(F32) * grad_ref[...][None]
    spectrum = dot(left_parts(product.reshape(GROUP * 256, 512)), table_ref[...])
    combos = []
    for m in range(GROUP):
        out = dot(spread_ref[...], right_parts(spectrum[m * 256 : m * 256 + 256]))
        combos += [out[k * 16 : k * 16 + 16] for k in range(modes)]
    for jh in range(2):
        pieces = [c[:, jh * LANES : (jh + 1) * LANES] for c in combos]
        powers = [
            power_of(jnp.concatenate([peak(pieces[8 * t + c]) for t in range(tiles)], axis=0))
            for c in range(8)
        ]
        shrink = [jnp.exp2(-p) for p in powers]
        for t in range(tiles):
            codes = [to_code(pieces[8 * t + c] * shrink[c][t : t + 1]) for c in range(8)]
            for j, code in enumerate(regroup(codes, 16)):
                message_ref[jh * 8 + j, step * tiles + t] = code
        for j, power in enumerate(regroup(powers, 16)):
            power_ref[jh * 8 + j, step, 0:tiles, :] = power

    @pl.when(step == steps - 1)
    def _():
        store_powers(power_ref, message_ref, message_ref.shape[1] - power_ref.shape[1] // 2)


def spectral(
    tiles, modes, member_scale, retained_ref, offset_ref, message_ref, weight_ref, back_table_ref,
    table_ref, *rest,
):
    control_ref, back_ref, band_ref, scale_ref, power_ref = rest[-5:]
    step = pl.program_id(0)
    steps = pl.num_programs(0)
    groups = power_ref.shape[1]
    first_tail = message_ref.shape[1] - groups // 2

    @pl.when(step == 0)
    def _():
        for i in range(16):
            for t in range(groups // 2):
                scale = jnp.exp2(from_code(message_ref[i, first_tail + t]))
                scale_ref[i, 2 * t] = scale[0:8]
                scale_ref[i, 2 * t + 1] = scale[8:16]
        power_ref[...] = jnp.zeros_like(power_ref)
        wave = (
            lax.broadcasted_iota(jnp.int32, (16, LANES), 0)
            + lax.broadcasted_iota(jnp.int32, (16, LANES), 1)
            + offset_ref[0]
        )
        bands = [jnp.where(wave < retained_ref[k], weight_ref[k], 0.0) for k in range(modes)]
        for t in range(tiles):
            tile = jnp.concatenate([bands[(8 * t + c) % modes] for c in range(8)], axis=0)
            band_ref[:, t * LANES : (t + 1) * LANES] = tile.T

    if modes < 16:
        control_ref[:, modes:] = jnp.zeros((GROUP, 16 - modes, 16, LANES), F32)
    lines = []
    for t in range(tiles):
        code = from_code(message_ref[:, step * tiles + t])
        lines.append((code * scale_ref[:, step, t : t + 1, :]).reshape(256, LANES))
    band = band_ref[...]
    control = dot(table_ref[...], right_parts(jnp.concatenate(lines, axis=1)))
    control = control * (band * member_scale)
    back = dot(back_table_ref[...], right_parts(control * band))
    for t in range(tiles):
        turned = control[:, t * LANES : (t + 1) * LANES].T
        for c in range(8):
            m, k = divmod(8 * t + c, modes)
            control_ref[m, k] = turned[16 * c : 16 * c + 16]
    for i in range(16):
        pieces = [
            back[16 * i : 16 * i + 16, t * LANES : (t + 1) * LANES] for t in range(tiles)
        ]
        power = power_of(jnp.concatenate([peak(p) for p in pieces], axis=0))
        shrink = jnp.exp2(-power)
        for t in range(tiles):
            back_ref[i, step * tiles + t] = to_code(pieces[t] * shrink[t : t + 1])
        power_ref[i, step, 0:tiles, :] = power

    @pl.when(step == steps - 1)
    def _():
        store_powers(power_ref, back_ref, first_tail)


def backward_rows(
    tiles, modes, member_scale, first, mode_count_ref, members_ref, back_ref, basis_ref, table_ref,
    *rest,
):
    if first:
        total_ref, spread_ref, scale_ref = rest
    else:
        before_ref, total_ref, spread_ref, scale_ref = rest
    step = pl.program_id(0)
    groups = scale_ref.shape[2]
    first_tail = back_ref.shape[1] - groups // 2

    @pl.when(step == 0)
    def _():
        basis = masked_basis(basis_ref, mode_count_ref, 1) * member_scale
        spread_ref[...] = spread(basis, 256, modes * 16)
        for jh in range(2):
            for t in range(groups // 2):
                scales = regroup(
                    [jnp.exp2(from_code(back_ref[jh * 8 + j, first_tail + t])) for j in range(8)],
                    16,
                )
                for c in range(8):
                    scale_ref[jh, c, 2 * t] = scales[c][0:8]
                    scale_ref[jh, c, 2 * t + 1] = scales[c][8:16]
        if first:
            total_ref[...] = jnp.zeros_like(total_ref)
        else:
            total_ref[...] = before_ref[...]

    halves = []
    for jh in range(2):
        combos = []
        scales = [scale_ref[jh, c, step] for c in range(8)]
        for t in range(tiles):
            codes = [back_ref[jh * 8 + j, step * tiles + t] for j in range(8)]
            for c, code in enumerate(regroup(codes, 16)):
                combos.append(from_code(code) * scales[c][t : t + 1])
        halves.append(combos)
    levels = []
    for m in range(GROUP):
        rows = [
            jnp.concatenate(half[m * modes : (m + 1) * modes], axis=0) for half in halves
        ]
        levels.append(dot(spread_ref[...], right_parts(jnp.concatenate(rows, axis=1))))
    vertical = dot(left_parts(jnp.concatenate(levels, axis=0)), table_ref[...])
    values = members_ref[...].astype(F32) * vertical.reshape(GROUP, 16, 16, 512)
    total_ref[...] += jnp.sum(values, axis=0)


def whole(shape):
    return pl.BlockSpec(shape, lambda m: (0,) * len(shape))


SMEM = pl.BlockSpec(memory_space=pltpu.SMEM)


def call(kernel, name, steps, operands, in_specs, out_specs, out_shape, scratch, flops, **more):
    return pl.pallas_call(
        kernel,
        grid=(steps,),
        in_specs=in_specs,
        out_specs=out_specs,
        out_shape=out_shape,
        scratch_shapes=scratch,
        compiler_params=pltpu.CompilerParams(
            dimension_semantics=("arbitrary",), vmem_limit_bytes=VMEM_LIMIT
        ),
        cost_estimate=pl.CostEstimate(
            flops=steps * flops, bytes_accessed=steps * flops // 100, transcendentals=0
        ),
        name=name,
        **more,
    )(*operands)


def stacked(table, axis, order):
    both = table_parts(table)
    return jnp.asarray(np.concatenate([both[i] for i in order], axis=axis))


def tables():
    x_table, y_table = cosine_table(512, 256), cosine_table(256, 128)
    return (
        stacked(x_table, 0, (0, 0, 1)),
        stacked(y_table.T, 1, (0, 1, 0)),
        stacked(y_table, 1, (0, 1, 0)),
        stacked(x_table.T, 0, (0, 0, 1)),
    )


def sizes(modes, count):
    groups = count // GROUP
    tiles = modes * GROUP // 8
    padded = groups + groups % 2
    shape = (16, groups * tiles + padded // 2, 16, LANES)
    return groups, tiles, padded, jax.ShapeDtypeStruct(shape, jnp.int16)


def member_block(chunk, groups):
    return pl.BlockSpec((GROUP, 16, 16, 512), lambda m: (m + chunk * groups, 0, 0, 0))


def run_forward(modes, count, chunk, mode_count, members, levels, basis_t, table):
    groups, tiles, padded, message = sizes(modes, count)
    return call(
        functools.partial(forward_rows, tiles, modes), "forward_rows", groups,
        (mode_count, members, levels, basis_t, table),
        [SMEM, member_block(chunk, groups)] + [whole(a.shape) for a in (levels, basis_t, table)],
        whole(message.shape), message,
        [pltpu.VMEM((modes * 16, 768), BF16), pltpu.VMEM((16, padded, 8, LANES), F32)],
        1_600_000_000,
    )


def run_spectral(
    modes, count, chunk, held, member_scale, retained, offset, message, weight, back_table, table,
    control,
):
    groups, tiles, padded, kind = sizes(modes, count)
    extra = [] if control is None else [control]
    return call(
        functools.partial(spectral, tiles, modes, member_scale), "spectral", groups,
        [retained, offset, message, weight, back_table, table] + extra,
        [SMEM, SMEM]
        + [whole(a.shape) for a in (message, weight, back_table, table)]
        + [pl.BlockSpec(memory_space=pl.ANY)] * len(extra),
        [
            pl.BlockSpec((GROUP, 16, 16, LANES), lambda m: (m + chunk * groups, 0, 0, 0)),
            whole(kind.shape),
        ],
        [jax.ShapeDtypeStruct((held, 16, 16, LANES), F32), kind],
        [pltpu.VMEM((LANES, tiles * LANES), F32)]
        + [pltpu.VMEM((16, padded, 8, LANES), F32)] * 2,
        1_000_000_000,
        input_output_aliases={6: 0} if extra else {},
    )


def run_backward(
    modes, count, chunk, member_scale, mode_count, members, back, basis, table, total
):
    groups, tiles, padded, _ = sizes(modes, count)
    extra = [] if total is None else [total]
    return call(
        functools.partial(backward_rows, tiles, modes, member_scale, total is None),
        "backward_rows", groups,
        [mode_count, members, back, basis, table] + extra,
        [SMEM, member_block(chunk, groups)]
        + [whole(a.shape) for a in [back, basis, table] + extra],
        whole((16, 16, 512)), jax.ShapeDtypeStruct((16, 16, 512), F32),
        [
            pltpu.VMEM((256, modes * 48), BF16),
            pltpu.VMEM((2, 8, padded, 8, LANES), F32),
        ],
        1_600_000_000,
    )


def local(gradient, members, eof_basis, spectral_weight, retained, mode_count):
    group_count = lax.axis_size("mem")
    held, share = members.shape[0], gradient.shape[0]
    member_scale = 1.0 / math.sqrt(held * group_count - 1)
    x_forward, y_forward, y_back, x_back = tables()
    copies = jnp.broadcast_to(gradient[None], (group_count,) + gradient.shape)
    levels = lax.all_to_all(copies, "mem", 0, 0, tiled=True).reshape(16, 16, 512)
    offset = (lax.axis_index("grid") * 16).astype(jnp.int32).reshape(1)
    weight = spectral_weight.transpose(0, 2, 1)
    basis_t = eof_basis.T
    modes, count = 16, held // CHUNKS

    messages, backs = [], []
    control = total = None
    for chunk in range(CHUNKS):
        message = run_forward(
            modes, count, chunk, mode_count, members, levels, basis_t, x_forward
        )
        messages.append(lax.all_to_all(message, "grid", 0, 0, tiled=True))
    for chunk in range(CHUNKS):
        control, back = run_spectral(
            modes, count, chunk, held, member_scale, retained, offset, messages[chunk], weight,
            y_back, y_forward, control,
        )
        backs.append(lax.all_to_all(back, "grid", 0, 0, tiled=True))
    for chunk in range(CHUNKS):
        total = run_backward(
            modes, count, chunk, member_scale, mode_count, members, backs[chunk], eof_basis,
            x_back, total,
        )
    blocks = total.reshape(group_count, share, 16, 512)
    increment = jnp.sum(lax.all_to_all(blocks, "mem", 0, 0, tiled=True), axis=0)
    return (increment, control.transpose(0, 1, 3, 2))


def solution(mesh):
    return jax.shard_map(
        local,
        mesh=mesh,
        in_specs=(
            P("mem", "grid", None),
            P("mem", None, "grid", None),
            P(),
            P(None, None, "grid"),
            P(),
            P(),
        ),
        out_specs=(P("mem", "grid", None), P("mem", None, None, "grid")),
        check_vma=False,
    )
```

time: 948 us -> 133 us (0.14)
  waiting for transfers between devices: 717 us -> 39.4 us
  matrix products: 71.3 us -> 0 us
  local copies, waits for them, and re-layouts: 41 us -> 4.99 us
  Pallas kernels: 0 us -> 26.7 us
  blocking collectives: 67.2 us -> 46.6 us
  other arithmetic: 19.1 us -> 0.67 us
  between operations: 14.9 us -> 1.34 us
    reduce_scatter x1 -> x0, waiting for transfers between devices: 634 us -> none  [local(): lax.psum_scatter(blocks, ('mem', 'grid'), scatter_dimension=0, tiled=True)]
    dot_general x6 -> x0, matrix products: 71.3 us -> none  [the longest x1 17.2 us: local(): projected = jnp.einsum('zk,mzyx->mkyx', basis, product, precision=high)]
    all_gather x1 -> x0, blocking collectives: 32.5 us -> none  [local(): levels = lax.all_gather(gradient, 'mem', axis=0, tiled=True)]
    pallas_call x0 -> x3, Pallas kernels: none -> 26.7 us  [call(): pl.pallas_call(kernel, grid=(steps,), in_specs=in_specs, out_specs=out_sp...]
    all_gather x2 -> x0, waiting for transfers between devices: 26.6 us -> none  [the longest x1 24.3 us: local(): whole_grad = lax.all_gather(levels, 'grid', axis=1, tiled=True)]
    all_to_all x1 -> x2, waiting for transfers between devices: 56.5 us -> 39.4 us  [the longest x1 30.7 us: local(): messages.append(lax.all_to_all(message, 'grid', 0, 0, tiled=True))]
    all_to_all x1 -> x2, blocking collectives: 34.7 us -> 46.6 us  [the longest x1 33.8 us: local(): backs.append(lax.all_to_all(back, 'grid', 0, 0, tiled=True))]
    transpose x1 -> x0, local copies, waits for them, and re-layouts: 11.5 us -> none  [local(): blocks.transpose(0, 2, 1, 3, 4)]
  transfers between devices with their start and end apart: 4 -> 2, of which waited for: 4 -> 2; matrix products, arithmetic and copies ran while one was open for 7% -> 1% of each run, Pallas kernels for 0% -> 0%
where the time goes in v2:
time: 133 us
  blocking collectives  46.6 us (35%)
  waiting for transfers between devices  39.4 us (30%)
  Pallas kernels  26.7 us (20%)
  starting transfers between devices  13.2 us (10%)
  local copies, waits for them, and re-layouts  4.99 us (4%)
  between operations  1.34 us (1%)
    all_to_all x1, blocking collectives, local(): backs.append(lax.all_to_all(back, 'grid', 0, 0, tiled=True))  33.8 us
    all_to_all x1, waiting for transfers between devices, local(): messages.append(lax.all_to_all(message, 'grid', 0, 0, tiled=True))  30.7 us
    pallas_call x3, Pallas kernels, call(): pl.pallas_call(kernel, grid=(steps,), in_specs=in_specs, out_specs=out_sp...  26.7 us
    all_to_all x1, blocking collectives, local(): increment = jnp.sum(lax.all_to_all(blocks, 'mem', 0, 0, tiled=True), axis=0)  12.8 us
    all_to_all x1, waiting for transfers between devices, local(): lax.all_to_all(copies, 'mem', 0, 0, tiled=True).reshape(16, 16, 512)  8.66 us
    all_to_all x1, starting transfers between devices, local(): messages.append(lax.all_to_all(message, 'grid', 0, 0, tiled=True))  7.72 us
    all_to_all x1, starting transfers between devices, local(): lax.all_to_all(copies, 'mem', 0, 0, tiled=True).reshape(16, 16, 512)  5.48 us
    unnamed x17, local copies, waits for them, and re-layouts  3.29 us
  transfers between devices with their start and end apart: 2, of which 2 were waited for; matrix products, arithmetic and copies ran while one was open for 1% of the time, Pallas kernels for 0%

profile of v2, /device:TPU:0, one launch (start us, length us, event | category | flops | bytes accessed | tf_op | source)
XLA Modules:
  0.0 132.8 jit_solution(14663249544000179197)
XLA Ops:
  0.6 1.7 %broadcast_in_dim.2 = f32[8,2,16,512]{3,2,1,0:T(8,128)} broadcast(f32[2,16,512]{2,1,0:T(8,128)} %param.10), dimensions={1,2,3} | broadcast | bytes 589824 | tf_op jit(solution)/shard_map/broadcast_in_dim | solution.py:380
  2.3 5.5 %all-to-all-start = ((f32[8,2,16,512]{3,2,1,0:T(8,128)}), f32[8,2,16,512]{3,2,1,0:T(8,128)S(1)}, u32[]{:S(2)}, u32[]{:S(2)}) async-start(f32[8,2,16,512]{3,2,1,0:T(8,128)} %broadcast_in_dim.2), calls=%async_computation | async-start | bytes 1048576 | tf_op jit(solution)/shard_map/all_to_all | solution.py:381
  8.5 0.8 copy.12
  9.2 8.7 %all-to-all-done = f32[8,2,16,512]{3,2,1,0:T(8,128)S(1)} async-done(((f32[8,2,16,512]{3,2,1,0:T(8,128)}), f32[8,2,16,512]{3,2,1,0:T(8,128)S(1)}, u32[]{:S(2)}, u32[]{:S(2)}) %all-to-all-start) | async-done | bytes 524320 | tf_op jit(solution)/shard_map/all_to_all | solution.py:381
  17.9 0.0 copy-start.5
  17.9 1.1 copy-done.5
  19.0 12.2 %forward_rows.1 = s16[16,34,16,128]{3,2,1,0:T(8,128)(2,1)S(1)} custom-call(s32[1]{0:T(128)S(6)} %copy.13.mode_count_ref, bf16[16,16,16,512]{3,2,1,0:T(8,128)(2,1)} %members_ref.3, f32[16,16,512]{2,1,0:T(8,128)S(1)} %bitcast.6, f32[16,16]{1,0:T(8,128)S(1)} %bitcast.8, bf16[1536,256]{1,0:T(8,128)(2,1)S(1)} %copy-done.5), custom_call_target="tpu_custom_call" | custom-call | flops 6400000000 | bytes 64000000 | tf_op jit(solution)/shard_map/forward_rows/pallas_call | solution.py:274
  31.3 0.0 copy-start
  31.3 1.4 %copy-done = s16[16,34,16,128]{3,2,1,0:T(8,128)(2,1)} copy-done((s16[16,34,16,128]{3,2,1,0:T(8,128)(2,1)}, s16[16,34,16,128]{3,2,1,0:T(8,128)(2,1)S(1)}, u32[]{:S(2)}) %copy-start) | copy-done | bytes 2228248
  32.7 0.0 copy-start.2
  32.7 0.0 copy-start.3
  32.7 7.7 %all-to-all-start.1 = ((s16[16,34,16,128]{3,2,1,0:T(8,128)(2,1)}), s16[16,34,16,128]{3,2,1,0:T(8,128)(2,1)S(1)}, u32[]{:S(2)}, u32[]{:S(2)}) async-start(s16[16,34,16,128]{3,2,1,0:T(8,128)(2,1)} %copy-done), calls=%async_computation.1 | async-start | bytes 4456448 | tf_op jit(solution)/shard_map/all_to_all | solution.py:393
  40.4 30.7 %all-to-all-done.1.message_ref = s16[16,34,16,128]{3,2,1,0:T(8,128)(2,1)S(1)} async-done(((s16[16,34,16,128]{3,2,1,0:T(8,128)(2,1)}), s16[16,34,16,128]{3,2,1,0:T(8,128)(2,1)S(1)}, u32[]{:S(2)}, u32[]{:S(2)}) %all-to-all-start.1) | async-done | bytes 2228256 | tf_op jit(solution)/shard_map/all_to_all | solution.py:393
  71.1 0.0 copy-done.2
  71.1 0.0 copy-done.3
  71.1 0.0 copy-done.6
  71.1 0.0 copy-done.7
  71.1 5.7 %spectral.1 = (f32[16,16,16,128]{3,2,1,0:T(8,128)}, s16[16,34,16,128]{3,2,1,0:T(8,128)(2,1)S(1)}) custom-call(s32[16]{0:T(128)S(1)} %copy-done.3, s32[1]{0:T(128)} %bitcast.offset_ref, s16[16,34,16,128]{3,2,1,0:T(8,128)(2,1)S(1)} %all-to-all-done.1.message_ref, f32[16,16,128]{2,1,0:T(8,128)S(1)} %bitcast.9, bf16[256,384]{1,0:T(8,128)(2,1)S(1)} %copy-done.6, ...), custom_call_target="tpu_custom_call" | custom-call | flops 4000000000 | bytes 40000000 | tf_op jit(solution)/shard_map/spectral/pallas_call | solution.py:274
  76.8 33.8 %all_to_all.20.back_ref = s16[16,34,16,128]{3,2,1,0:T(8,128)(2,1)S(1)} all-to-all(s16[16,34,16,128]{3,2,1,0:T(8,128)(2,1)S(1)} %get-tuple-element.4), channel_id=1, replica_groups=mesh['mem'=8,'grid'=16] {'grid'}, dimensions={0} | all-to-all | bytes 4456448 | tf_op jit(solution)/shard_map/all_to_all | solution.py:399
  110.6 0.0 copy-done.1
  110.6 0.0 copy-done.4
  110.6 8.8 %backward_rows.1 = f32[16,16,512]{2,1,0:T(8,128)S(1)} custom-call(s32[1]{0:T(128)S(6)} %copy.13.mode_count_ref, bf16[16,16,16,512]{3,2,1,0:T(8,128)(2,1)} %members_ref.3, s16[16,34,16,128]{3,2,1,0:T(8,128)(2,1)S(1)} %all_to_all.20.back_ref, f32[16,16]{1,0:T(8,128)S(1)} %copy-done.1, bf16[768,512]{1,0:T(8,128)(2,1)S(1)} %copy-done.4), custom_call_target="tpu_custom_call" | custom-call | flops 6400000000 | bytes 64000000 | tf_op jit(solution)/shard_map/backward_rows/pallas_call | solution.py:274
  119.4 12.8 %all_to_all.21 = f32[8,2,16,512]{3,2,1,0:T(8,128)S(1)} all-to-all(f32[8,2,16,512]{3,2,1,0:T(8,128)S(1)} %bitcast.7), channel_id=1, replica_groups=mesh['mem'=8,'grid'=16] {'mem'}, dimensions={0} | all-to-all | bytes 1048576 | tf_op jit(solution)/shard_map/all_to_all | solution.py:406
  132.2 0.7 reduce_sum.9
  (4 shorter events, 0.0 us)
Async XLA Ops:
  2.3 15.6 %all-to-all-start = ((f32[8,2,16,512]{3,2,1,0:T(8,128)}), f32[8,2,16,512]{3,2,1,0:T(8,128)S(1)}, u32[]{:S(2)}, u32[]{:S(2)}) async-start(f32[8,2,16,512]{3,2,1,0:T(8,128)} %broadcast_in_dim.2), calls=%async_computation | async-start | bytes 1048576 | tf_op jit(solution)/shard_map/all_to_all | solution.py:381
  17.9 1.1 copy-start.5
  31.3 1.4 %copy-start = (s16[16,34,16,128]{3,2,1,0:T(8,128)(2,1)}, s16[16,34,16,128]{3,2,1,0:T(8,128)(2,1)S(1)}, u32[]{:S(2)}) copy-start(s16[16,34,16,128]{3,2,1,0:T(8,128)(2,1)S(1)} %forward_rows.1) | copy-start | bytes 6684676
  32.7 38.5 %copy-start.2 = (f32[16,128,16]{1,2,0:T(8,128)S(1)}, f32[16,128,16]{1,2,0:T(8,128)}, u32[]{:S(2)}) copy-start(f32[16,128,16]{1,2,0:T(8,128)} %param.13) | copy-start | bytes 393220
  32.7 38.5 %copy-start.3 = (s32[16]{0:T(128)S(1)}, s32[16]{0:T(128)}, u32[]{:S(2)}) copy-start(s32[16]{0:T(128)} %retained_ref.1) | copy-start | bytes 196
  32.7 38.5 %copy-start.6 = (bf16[256,384]{1,0:T(8,128)(2,1)S(1)}, bf16[256,384]{1,0:T(8,128)(2,1)}, u32[]{:S(2)}) copy-start(bf16[256,384]{1,0:T(8,128)(2,1)} %constant.18.clone.back_table_ref) | copy-start | bytes 589828
  32.7 38.5 %copy-start.7 = (bf16[128,768]{1,0:T(8,128)(2,1)S(1)}, bf16[128,768]{1,0:T(8,128)(2,1)}, u32[]{:S(2)}) copy-start(bf16[128,768]{1,0:T(8,128)(2,1)} %constant.17.clone.table_ref) | copy-start | bytes 589828
  32.7 38.4 %all-to-all-start.1 = ((s16[16,34,16,128]{3,2,1,0:T(8,128)(2,1)}), s16[16,34,16,128]{3,2,1,0:T(8,128)(2,1)S(1)}, u32[]{:S(2)}, u32[]{:S(2)}) async-start(s16[16,34,16,128]{3,2,1,0:T(8,128)(2,1)} %copy-done), calls=%async_computation.1 | async-start | bytes 4456448 | tf_op jit(solution)/shard_map/all_to_all | solution.py:393
  76.8 33.8 %copy-start.1 = (f32[16,16]{1,0:T(8,128)S(1)}, f32[16,16]{1,0:T(8,128)}, u32[]{:S(2)}) copy-start(f32[16,16]{1,0:T(8,128)} %basis_ref.1) | copy-start | bytes 3076
  76.8 33.8 %copy-start.4 = (bf16[768,512]{1,0:T(8,128)(2,1)S(1)}, bf16[768,512]{1,0:T(8,128)(2,1)}, u32[]{:S(2)}) copy-start(bf16[768,512]{1,0:T(8,128)(2,1)} %constant.19.clone.table_ref) | copy-start | bytes 2359300
